TPU v7x, 32 devices: a whole 2x2x4 slice. The times are simulated.
32 devices in a mesh: lat: 4 (over x, core), lon: 8 (over z, y).
Axes of the slice: x: 2, y: 2, z: 4, core: 2. Of those that a mesh axis runs over, the one named last changes fastest.
Arguments:
- fields: float32 [4, 90, 64, 1024], P(None, None, 'lat', 'lon'), may hold values from -6 to 6
- courant_lon: float32 [90, 64, 1024], P(None, 'lat', 'lon'), may hold values from -0.3 to 0.3
- courant_lat: float32 [90, 64, 1024], P(None, 'lat', 'lon'), may hold values from -0.3 to 0.3
- diffusion: float32 [90, 64, 1024], P(None, 'lat', 'lon'), may hold values from 0.1 to 0.24
- tend_cot: bfloat16 [4, 90, 64, 1024], P(None, None, 'lat', 'lon'), may hold values from -6 to 6
- col_list: int32 [4, 8, 1024], P('lat', 'lon'), may hold values from 0 to 2047, as said below
- block_count: int32 [4, 8, 8], P('lat', 'lon'), may hold values from 1 to 128, as said below
- block_dest: int32 [4, 8, 8], P('lat', 'lon'), may hold values from 0 to 7, each once within a row
- w_in: bfloat16 [8, 360, 512], P('lon', None, 'lat'), may hold values from -0.3125 to 0.3125
- w_mid: bfloat16 [8, 512, 512], P('lon', None, 'lat'), may hold values from -0.25 to 0.25
- w_out: bfloat16 [8, 360, 512], P('lon', None, 'lat'), may hold values from -0.25 to 0.25
Outputs:
- new_fields: float32 [4, 90, 64, 1024], P(None, None, 'lat', 'lon')
- adjoint: bfloat16 [4, 90, 64, 1024], P(None, None, 'lat', 'lon')
- grad_in: float32 [8, 360, 512], P('lon', None, 'lat')
- grad_mid: float32 [8, 512, 512], P('lon', None, 'lat')
- grad_out: float32 [8, 360, 512], P('lon', None, 'lat')
Inputs may be any that keep to these rules, and one draw needn't show every extreme that they name: `col_list`: within one tile's list no local column appears twice. `block_count`: in each tile one block has all 128 slots live. `block_dest`: each tile's row names every expert exactly once.
All inputs are finite; a program needn't handle non-finite values.
Results may differ from a plain program's by a relative error of at most 0.0074.
Values may be sent and summed in bfloat16 or wider, within the bound.
A program may use at most 320 MiB of HBM per device.

v0:
```python
import jax
import jax.numpy as jnp
from jax import lax
from jax.sharding import PartitionSpec as P

STEPS = 4


def extended(array, sides, width):
    for axis, dim in sides:
        size, length = (lax.axis_size(axis), array.shape[dim])
        up = [(i, (i + 1) % size) for i in range(size)]
        down = [(j, i) for i, j in up]
        last = lax.slice_in_dim(array, length - width, length, axis=dim)
        first = lax.slice_in_dim(array, 0, width, axis=dim)
        before = lax.ppermute(last, axis, up)
        after = lax.ppermute(first, axis, down)
        array = jnp.concatenate([before, array, after], axis=dim)
    return array


def dsilu(value):
    sig = jax.nn.sigmoid(value)
    return sig * (1.0 + value * (1.0 - sig))


def physics(x, g, weights):
    w_first, w_second, w_third = weights
    lead = "e"
    xf = x.astype(jnp.float32)
    scale = lax.rsqrt(jnp.mean(xf * xf, axis=0, keepdims=True) + 1e-06)
    xn = (xf * scale).astype(jnp.bfloat16)
    a_one = jnp.einsum(lead + "fh,fbc->hbc", w_first, xn, preferred_element_type=jnp.float32)
    h_one = jax.nn.silu(a_one).astype(jnp.bfloat16)
    a_two = jnp.einsum(lead + "gh,gbc->hbc", w_second, h_one, preferred_element_type=jnp.float32)
    h_two = jax.nn.silu(a_two).astype(jnp.bfloat16)
    tend = jnp.einsum(
        lead + "fh,hbc->fbc", w_third, h_two, preferred_element_type=jnp.float32
    ).astype(jnp.bfloat16)
    back_two = jnp.einsum(lead + "fh,fbc->hbc", w_third, g, preferred_element_type=jnp.float32)
    d_two = (back_two * dsilu(a_two)).astype(jnp.bfloat16)
    back_one = jnp.einsum(lead + "gh,hbc->gbc", w_second, d_two, preferred_element_type=jnp.float32)
    d_one = (back_one * dsilu(a_one)).astype(jnp.bfloat16)
    d_norm = jnp.einsum(lead + "fh,hbc->fbc", w_first, d_one, preferred_element_type=jnp.float32)
    adj = (
        scale * d_norm - xf * (scale * scale * scale) * jnp.mean(xf * d_norm, axis=0, keepdims=True)
    ).astype(jnp.bfloat16)
    out_form = "fh"
    mid_form = "gh"
    grad_first = jnp.einsum("fbc,hbc->" + out_form, xn, d_one, preferred_element_type=jnp.float32)
    grad_second = jnp.einsum(
        "gbc,hbc->" + mid_form, h_one, d_two, preferred_element_type=jnp.float32
    )
    grad_third = jnp.einsum("fbc,hbc->" + out_form, g, h_two, preferred_element_type=jnp.float32)
    return (tend, adj, (grad_first[None], grad_second[None], grad_third[None]))


def update(state, c_lon, c_lat, c_dif, east, west, north, south):
    return (
        state
        - 0.5 * c_lon * (east - west)
        - 0.5 * c_lat * (north - south)
        + c_dif * (east + west + north + south - 4.0 * state)
    )


def shards(
    fields,
    courant_lon,
    courant_lat,
    diffusion,
    tend_cot,
    col_list,
    block_count,
    block_dest,
    w_in,
    w_mid,
    w_out,
):
    nfield, levels, rows, columns = fields.shape
    feat = nfield * levels
    ncol = rows * columns
    total_rows = rows * lax.axis_size("lat")
    first_row = lax.axis_index("lat") * rows
    nblock = block_dest.shape[-1]
    block_len = col_list.shape[-1] // nblock
    dest = block_dest.reshape(nblock)
    counts = block_count.reshape(nblock)
    order = jnp.zeros((nblock,), jnp.int32).at[dest].set(jnp.arange(nblock, dtype=jnp.int32))
    slots = col_list.reshape(nblock, block_len)[order]
    live = jnp.arange(block_len, dtype=jnp.int32)[None, :] < counts[order][:, None]
    col_data = fields.astype(jnp.bfloat16).reshape(feat, ncol)
    cot_data = tend_cot.reshape(feat, ncol)
    picked_x = col_data[:, slots]
    picked_g = cot_data[:, slots]
    send_x = jnp.where(live[None], picked_x, jnp.zeros_like(picked_x))
    send_g = jnp.where(live[None], picked_g, jnp.zeros_like(picked_g))
    weights = (
        lax.all_gather(w_in, "lat", axis=2, tiled=True),
        lax.all_gather(w_mid, "lat", axis=2, tiled=True),
        lax.all_gather(w_out, "lat", axis=2, tiled=True),
    )
    recv_x, recv_g = (
        lax.all_to_all(send_x, "lon", split_axis=1, concat_axis=1, tiled=True),
        lax.all_to_all(send_g, "lon", split_axis=1, concat_axis=1, tiled=True),
    )
    tend, adj, grads = physics(recv_x, recv_g, weights)
    back_tend, back_adj = (
        lax.all_to_all(tend, "lon", split_axis=1, concat_axis=1, tiled=True),
        lax.all_to_all(adj, "lon", split_axis=1, concat_axis=1, tiled=True),
    )
    state = fields
    lane = jnp.arange(columns, dtype=jnp.int32)[None, :]
    row_index = jnp.arange(rows, dtype=jnp.int32)[:, None]
    top_inside = (first_row + rows < total_rows).astype(jnp.float32)
    bottom_inside = (first_row > 0).astype(jnp.float32)
    for step in range(STEPS):
        padded = extended(state.astype(jnp.bfloat16), (("lat", 2), ("lon", 3)), 1).astype(
            state.dtype
        )
        east_rim = padded[:, :, 1:-1, -1:]
        west_rim = padded[:, :, 1:-1, :1]
        north_rim = padded[:, :, -1:, 1:-1] * top_inside
        south_rim = padded[:, :, :1, 1:-1] * bottom_inside
        east = jnp.where(lane == columns - 1, east_rim, jnp.roll(state, -1, axis=3))
        west = jnp.where(lane == 0, west_rim, jnp.roll(state, 1, axis=3))
        north = jnp.where(row_index == rows - 1, north_rim, jnp.roll(state, -1, axis=2))
        south = jnp.where(row_index == 0, south_rim, jnp.roll(state, 1, axis=2))
        state = update(state, courant_lon, courant_lat, diffusion, east, west, north, south)
    grad_in, grad_mid, grad_out = (
        lax.psum_scatter(grads[0], "lat", scatter_dimension=2, tiled=True),
        lax.psum_scatter(grads[1], "lat", scatter_dimension=2, tiled=True),
        lax.psum_scatter(grads[2], "lat", scatter_dimension=2, tiled=True),
    )
    flat = slots.reshape(-1)
    tend_cols = jnp.zeros((feat, ncol), jnp.bfloat16).at[:, flat].set(back_tend.reshape(feat, -1))
    adj_cols = jnp.zeros((feat, ncol), jnp.bfloat16).at[:, flat].set(back_adj.reshape(feat, -1))
    new_fields = state + tend_cols.astype(jnp.float32).reshape(fields.shape)
    adjoint = adj_cols.reshape(fields.shape)
    return (new_fields, adjoint, grad_in, grad_mid, grad_out)


def solution(mesh):
    return jax.shard_map(
        shards,
        mesh=mesh,
        in_specs=(
            P(None, None, "lat", "lon"),
            P(None, "lat", "lon"),
            P(None, "lat", "lon"),
            P(None, "lat", "lon"),
            P(None, None, "lat", "lon"),
            P("lat", "lon", None),
            P("lat", "lon", None),
            P("lat", "lon", None),
            P("lon", None, "lat"),
            P("lon", None, "lat"),
            P("lon", None, "lat"),
        ),
        out_specs=(
            P(None, None, "lat", "lon"),
            P(None, None, "lat", "lon"),
            P("lon", None, "lat"),
            P("lon", None, "lat"),
            P("lon", None, "lat"),
        ),
        check_vma=False,
    )
```

profile of v0, /device:TPU:0, one launch (start us, length us, event | category | flops | bytes accessed | tf_op | source)
XLA Modules:
  0.0 544.1 jit_solution(14581867227868549513)
XLA Ops:
  31.1 5.0 gather_fusion.2
  41.2 6.6 %all-to-all-start = ((bf16[360,8,128]{2,0,1:T(8,128)(2,1)}), bf16[360,8,128]{2,0,1:T(8,128)(2,1)}, u32[]{:S(2)}, u32[]{:S(2)}) async-start(bf16[360,8,128]{2,0,1:T(8,128)(2,1)} %get-tuple-element.98), calls=%async_computation | async-start | bytes 1474560 | tf_op jit(solution)/shard_map/all_to_all | solution.py:104
  59.5 6.3 %all_gather.9 = bf16[1,360,512]{2,1,0:T(8,128)(2,1)S(1)} all-gather(bf16[1,360,128]{2,1,0:T(8,128)(2,1)S(1)} %copy-done.54), channel_id=1, replica_groups=mesh['lat'=4,'lon'=8] {'lat'}, dimensions={2}, use_global_device_ids=true | all-gather | bytes 460800 | tf_op jit(solution)/shard_map/all_gather | solution.py:99
  65.9 6.9 %all_gather.11 = bf16[1,360,512]{2,1,0:T(8,128)(2,1)} all-gather(bf16[1,360,128]{2,1,0:T(8,128)(2,1)S(1)} %copy-done.55), channel_id=1, replica_groups=mesh['lat'=4,'lon'=8] {'lat'}, dimensions={2}, use_global_device_ids=true | all-gather | bytes 460800 | tf_op jit(solution)/shard_map/all_gather | solution.py:101
  72.8 8.0 %all_gather.10 = bf16[1,512,512]{2,1,0:T(8,128)(2,1)} all-gather(bf16[1,512,128]{2,1,0:T(8,128)(2,1)S(1)} %copy-done.53), channel_id=1, replica_groups=mesh['lat'=4,'lon'=8] {'lat'}, dimensions={2}, use_global_device_ids=true | all-gather | bytes 655360 | tf_op jit(solution)/shard_map/all_gather | solution.py:100
  101.2 5.3 copy.223
  124.0 11.5 %copy.128 = bf16[4,90,18,1]{3,0,2,1:T(4,128)(2,1)} copy(bf16[4,90,18,1]{1,0,3,2:T(4,128)(2,1)} %collective-permute-done.2) | data formatting | bytes 25920 | tf_op jit(solution)/shard_map/ppermute | solution.py:16
  138.0 7.1 %maximum_convert_fusion = f32[4,90,18,130]{3,0,2,1:T(4,128)S(1)} fusion(bf16[4,90,18,1]{3,0,2,1:T(4,128)(2,1)} %copy.129, bf16[4,90,1,128]{3,0,2,1:T(4,128)(2,1)} %collective-permute-done.1, bf16[4,90,16,128]{3,0,2,1:T(4,128)(2,1)} %copy-done.8, bf16[4,90,1,128]{3,0,2,1:T(4,128)(2,1)} %collective-permute-done, bf16[4,90,18,1]{3,0,2,1:T(4,128)(2,1)} %copy.128), kind=kLoop, calls=%fused_computation.7 | loop fusion | flops 8424000 | bytes 5054400 | tf_op jit(solution)/shard_map/convert_element_type | solution.py:118
  145.1 4.9 fusion.57
  150.0 10.6 %copy.195 = f32[4,90,16,1]{0,2,1,3:T(8,128)} copy(f32[4,90,16,1]{3,0,2,1:T(4,128)} %get-tuple-element.37) | data formatting | bytes 46080 | tf_op jit(solution)/shard_map/jit(_where)/broadcast_in_dim | solution.py:125
  160.5 10.6 %copy.196 = f32[4,90,16,1]{0,2,1,3:T(8,128)} copy(f32[4,90,16,1]{3,0,2,1:T(4,128)} %get-tuple-element.38) | data formatting | bytes 46080 | tf_op jit(solution)/shard_map/jit(_where)/broadcast_in_dim | solution.py:126
  173.7 11.9 %fusion.53 = (bf16[4,90,16,128]{3,0,2,1:T(4,128)(2,1)S(1)}, f32[4,90,16,128]{3,0,2,1:T(4,128)S(1)}) fusion(f32[90,16,128]{2,1,0:T(8,128)S(1)} %copy-done.32, f32[4,90,15,128]{3,0,2,1:T(4,128)} %copy.220, f32[4,90,1,128]{3,0,2,1:T(4,128)} %copy.221, f32[4,90,128]{2,0,1:T(4,128)S(1)} %get-tuple-element.46, pred[16]{0:T(512)(128)(4,1)S(1)} %get-tuple-element.105, ...), kind=kLoop, calls=%fused_computation.131 | loop fusion | flops 16220160 | bytes 21796128 | tf_op jit(solution)/shard_map/convert_element_type | solution.py:118
  215.1 5.0 collective-permute-done.6
  224.8 6.8 %maximum_convert_fusion.1 = f32[4,90,18,130]{3,0,2,1:T(4,128)S(1)} fusion(bf16[4,90,18,1]{3,0,2,1:T(4,128)(2,1)} %copy.147, bf16[4,90,1,128]{3,0,2,1:T(4,128)(2,1)} %copy-done.43, bf16[4,90,16,128]{3,0,2,1:T(4,128)(2,1)S(1)} %copy-done.14, bf16[4,90,1,128]{3,0,2,1:T(4,128)(2,1)} %copy-done.41, bf16[4,90,18,1]{3,0,2,1:T(4,128)(2,1)S(1)} %copy.146), kind=kLoop, calls=%fused_computation.8 | loop fusion | flops 8424000 | bytes 5054400 | tf_op jit(solution)/shard_map/convert_element_type | solution.py:118
  231.6 4.8 fusion.56
  236.4 10.6 %copy.197 = f32[4,90,16,1]{0,2,1,3:T(8,128)} copy(f32[4,90,16,1]{3,0,2,1:T(4,128)} %get-tuple-element.35) | data formatting | bytes 46080 | tf_op jit(solution)/shard_map/jit(_where)/broadcast_in_dim | solution.py:125
  247.0 10.6 %copy.198 = f32[4,90,16,1]{0,2,1,3:T(8,128)} copy(f32[4,90,16,1]{3,0,2,1:T(4,128)} %get-tuple-element.36) | data formatting | bytes 46080 | tf_op jit(solution)/shard_map/jit(_where)/broadcast_in_dim | solution.py:126
  260.1 12.4 %fusion.52 = (bf16[4,90,16,128]{3,0,2,1:T(4,128)(2,1)S(1)}, f32[4,90,16,128]{3,0,2,1:T(4,128)S(1)}) fusion(f32[4,90,16,128]{3,0,2,1:T(4,128)S(1)} %copy-done.7, f32[90,16,128]{2,1,0:T(8,128)S(1)} %copy-done.33, f32[4,90,15,128]{3,0,2,1:T(4,128)} %get-tuple-element.68, f32[4,90,1,128]{3,0,2,1:T(4,128)} %get-tuple-element.70, ...), kind=kLoop, calls=%fused_computation.130 | loop fusion | flops 16220160 | bytes 21796128 | tf_op jit(solution)/shard_map/convert_element_type | solution.py:118
  307.7 6.8 %maximum_convert_fusion.2 = f32[4,90,18,130]{3,0,2,1:T(4,128)S(1)} fusion(bf16[4,90,18,1]{3,0,2,1:T(4,128)(2,1)} %copy.155, bf16[4,90,1,128]{3,0,2,1:T(4,128)(2,1)} %copy-done.44, bf16[4,90,16,128]{3,0,2,1:T(4,128)(2,1)S(1)} %copy-done.12, bf16[4,90,1,128]{3,0,2,1:T(4,128)(2,1)} %copy-done.42, bf16[4,90,18,1]{3,0,2,1:T(4,128)(2,1)S(1)} %copy.154), kind=kLoop, calls=%fused_computation.9 | loop fusion | flops 8424000 | bytes 5054400 | tf_op jit(solution)/shard_map/convert_element_type | solution.py:118
  314.5 4.8 fusion.55
  319.3 10.6 %copy.199 = f32[4,90,16,1]{0,2,1,3:T(8,128)} copy(f32[4,90,16,1]{3,0,2,1:T(4,128)} %get-tuple-element.33) | data formatting | bytes 46080 | tf_op jit(solution)/shard_map/jit(_where)/broadcast_in_dim | solution.py:125
  329.9 10.6 %copy.200 = f32[4,90,16,1]{0,2,1,3:T(8,128)} copy(f32[4,90,16,1]{3,0,2,1:T(4,128)} %get-tuple-element.34) | data formatting | bytes 46080 | tf_op jit(solution)/shard_map/jit(_where)/broadcast_in_dim | solution.py:126
  343.0 12.4 %fusion.51 = (bf16[4,90,16,128]{3,0,2,1:T(4,128)(2,1)S(1)}, f32[4,90,16,128]{3,0,2,1:T(4,128)S(1)}) fusion(f32[4,90,16,128]{3,0,2,1:T(4,128)S(1)} %copy-done.5, f32[90,16,128]{2,1,0:T(8,128)S(1)} %copy-done.34, f32[4,90,15,128]{3,0,2,1:T(4,128)} %get-tuple-element.60, f32[4,90,1,128]{3,0,2,1:T(4,128)} %get-tuple-element.62, ...), kind=kLoop, calls=%fused_computation.129 | loop fusion | flops 16220160 | bytes 21796128 | tf_op jit(solution)/shard_map/convert_element_type | solution.py:118
  391.3 8.7 %maximum_convert_fusion.3 = f32[4,90,18,130]{3,0,2,1:T(4,128)} fusion(bf16[4,90,18,1]{3,0,2,1:T(4,128)(2,1)} %copy.163, bf16[4,90,1,128]{3,0,2,1:T(4,128)(2,1)} %copy-done.39, bf16[4,90,16,128]{3,0,2,1:T(4,128)(2,1)} %copy-done.10, bf16[4,90,1,128]{3,0,2,1:T(4,128)(2,1)S(1)} %collective-permute-done.12, bf16[4,90,18,1]{3,0,2,1:T(4,128)(2,1)} %copy.162), kind=kLoop, calls=%fused_computation.10 | loop fusion | flops 8424000 | bytes 5054400 | tf_op jit(solution)/shard_map/convert_element_type | solution.py:118
  411.6 11.3 %all-to-all-done.2 = bf16[360,8,128]{2,0,1:T(8,128)(2,1)} async-done(((bf16[360,8,128]{2,0,1:T(8,128)(2,1)}), bf16[360,8,128]{2,0,1:T(8,128)(2,1)}, u32[]{:S(2)}, u32[]{:S(2)}) %all-to-all-start.2) | async-done | bytes 737312 | tf_op jit(solution)/shard_map/all_to_all | solution.py:105
  445.3 6.1 %all-to-all-done.1 = bf16[360,8,128]{2,0,1:T(8,128)(2,1)} async-done(((bf16[360,8,128]{2,0,1:T(8,128)(2,1)}), bf16[360,8,128]{2,0,1:T(8,128)(2,1)}, u32[]{:S(2)}, u32[]{:S(2)}) %all-to-all-start.1) | async-done | bytes 737312 | tf_op jit(solution)/shard_map/all_to_all | solution.py:109
  455.7 7.2 %fusion.54 = (f32[4,90,16,1]{3,0,2,1:T(4,128)}, f32[4,90,16,1]{3,0,2,1:T(4,128)}) fusion(f32[4,90,18,130]{3,0,2,1:T(4,128)} %maximum_convert_fusion.3), kind=kLoop, calls=%fused_computation.132 | loop fusion | bytes 92160 | tf_op jit(solution)/shard_map/slice | solution.py:121
  462.9 10.6 %copy.201 = f32[4,90,16,1]{0,2,1,3:T(8,128)} copy(f32[4,90,16,1]{3,0,2,1:T(4,128)} %get-tuple-element.31) | data formatting | bytes 46080 | tf_op jit(solution)/shard_map/jit(_where)/broadcast_in_dim | solution.py:125
  473.5 10.6 %copy.202 = f32[4,90,16,1]{0,2,1,3:T(8,128)} copy(f32[4,90,16,1]{3,0,2,1:T(4,128)} %get-tuple-element.32) | data formatting | bytes 46080 | tf_op jit(solution)/shard_map/jit(_where)/broadcast_in_dim | solution.py:126
  496.5 7.0 %scatter_custom_fusion.2 = bf16[360,2048]{0,1:T(8,128)(2,1)} fusion(s32[1024]{0:T(1024)} %bitcast.203, bf16[1024,360]{1,0:T(8,128)(2,1)} %copy.182, bf16[]{:T(256)} %constant.23.clone.1), kind=kCustom, calls=%fused_computation.75 | custom fusion | bytes 1475072 | tf_op jit(solution)/shard_map/scatter | solution.py:137
  509.0 6.8 %scatter_custom_fusion.1 = bf16[360,2048]{0,1:T(8,128)(2,1)} fusion(s32[1024]{0:T(1024)} %bitcast.204, bf16[1024,360]{1,0:T(8,128)(2,1)} %copy.174, bf16[]{:T(256)} %constant.23.clone.1), kind=kCustom, calls=%fused_computation.77 | custom fusion | bytes 1475072 | tf_op jit(solution)/shard_map/scatter | solution.py:136
  523.2 12.2 %copy_add_fusion = f32[4,90,16,128]{3,0,2,1:T(4,128)S(1)} fusion(f32[4,90,16,128]{3,2,1,0:T(8,128)S(1)} %bitcast.187, f32[4,90,16,128]{3,0,2,1:T(4,128)S(1)} %get-tuple-element.26, f32[4,90,15,128]{3,0,2,1:T(4,128)} %get-tuple-element.52, f32[4,90,1,128]{3,0,2,1:T(4,128)} %get-tuple-element.54, f32[4,90,1,128]{3,0,2,1:T(4,128)S(1)} %copy-done.45, ...), kind=kLoop, calls=%fused_computation.27 | loop fusion | flops 16220160 | bytes 23270688 | tf_op jit(solution)/shard_map/add | solution.py:138
  (272 shorter events, 258.8 us)
Async XLA Ops:
  11.7 70.3 %collective-permute-start = (bf16[4,90,1,128]{3,0,2,1:T(4,128)(2,1)}, bf16[4,90,1,128]{3,0,2,1:T(4,128)(2,1)}, u32[]{:S(2)}, u32[]{:S(2)}) collective-permute-start(bf16[4,90,1,128]{3,0,2,1:T(4,128)(2,1)} %get-tuple-element.93), channel_id=1, source_target_pairs={{0,8},{8,16},{16,24},{24,0},{1,9},{9,17},{17,25},{25,1},{2,10},{10... | collective-permute-start | bytes 276488 | tf_op jit(solution)/shard_map/ppermute | solution.py:16
  12.1 69.8 %collective-permute-start.1 = (bf16[4,90,1,128]{3,0,2,1:T(4,128)(2,1)}, bf16[4,90,1,128]{3,0,2,1:T(4,128)(2,1)}, u32[]{:S(2)}, u32[]{:S(2)}) collective-permute-start(bf16[4,90,1,128]{3,0,2,1:T(4,128)(2,1)} %get-tuple-element.94), channel_id=1, source_target_pairs={{8,0},{16,8},{24,16},{0,24},{9,1},{17,9},{25,17},{1,25},{10,2},{18... | collective-permute-start | bytes 276488 | tf_op jit(solution)/shard_map/ppermute | solution.py:17
  41.2 358.7 %all-to-all-start = ((bf16[360,8,128]{2,0,1:T(8,128)(2,1)}), bf16[360,8,128]{2,0,1:T(8,128)(2,1)}, u32[]{:S(2)}, u32[]{:S(2)}) async-start(bf16[360,8,128]{2,0,1:T(8,128)(2,1)} %get-tuple-element.98), calls=%async_computation | async-start | bytes 1474560 | tf_op jit(solution)/shard_map/all_to_all | solution.py:104
  55.4 17.3 %copy-start.53 = (bf16[1,512,128]{2,1,0:T(8,128)(2,1)S(1)}, bf16[1,512,128]{2,1,0:T(8,128)(2,1)}, u32[]{:S(2)}) copy-start(bf16[1,512,128]{2,1,0:T(8,128)(2,1)} %param.20) | copy-start | bytes 393220
  55.4 25.3 %copy-start.46 = (f32[90,16,128]{2,1,0:T(8,128)S(1)}, f32[90,16,128]{2,1,0:T(8,128)}, u32[]{:S(2)}) copy-start(f32[90,16,128]{2,1,0:T(8,128)} %param.13) | copy-start | bytes 2211844
  55.4 25.3 %copy-start.47 = (f32[90,16,128]{2,1,0:T(8,128)S(1)}, f32[90,16,128]{2,1,0:T(8,128)}, u32[]{:S(2)}) copy-start(f32[90,16,128]{2,1,0:T(8,128)} %param.12) | copy-start | bytes 2211844
  58.9 23.1 %copy-start.9 = (bf16[4,90,16,128]{3,0,2,1:T(4,128)(2,1)S(1)}, bf16[4,90,16,128]{3,0,2,1:T(4,128)(2,1)}, u32[]{:S(2)}) copy-start(bf16[4,90,16,128]{3,0,2,1:T(4,128)(2,1)} %copy-done.8) | copy-start | bytes 4423684
  93.4 42.1 %collective-permute-start.3 = (bf16[4,90,18,1]{1,0,3,2:T(4,128)(2,1)S(1)}, bf16[4,90,18,1]{1,0,3,2:T(4,128)(2,1)S(1)}, u32[]{:S(2)}, u32[]{:S(2)}) collective-permute-start(bf16[4,90,18,1]{1,0,3,2:T(4,128)(2,1)S(1)} %copy.127), channel_id=1, source_target_pairs={{1,0},{2,1},{3,2},{4,3},{5,4},{6,5},{7,6},{0,7},{9,8},{10,9},{11,1... | collective-permute-start | bytes 38888 | tf_op jit(solution)/shard_map/ppermute | solution.py:17
  98.2 25.8 %collective-permute-start.2 = (bf16[4,90,18,1]{1,0,3,2:T(4,128)(2,1)}, bf16[4,90,18,1]{1,0,3,2:T(4,128)(2,1)}, u32[]{:S(2)}, u32[]{:S(2)}) collective-permute-start(bf16[4,90,18,1]{1,0,3,2:T(4,128)(2,1)} %copy.126), channel_id=1, source_target_pairs={{0,1},{1,2},{2,3},{3,4},{4,5},{5,6},{6,7},{7,0},{8,9},{9,10},{10,1... | collective-permute-start | bytes 38888 | tf_op jit(solution)/shard_map/ppermute | solution.py:16
  98.8 243.0 %copy-start.56 = (pred[16]{0:T(512)(128)(4,1)}, pred[16]{0:T(512)(128)(4,1)S(1)}, u32[]{:S(2)}) copy-start(pred[16]{0:T(512)(128)(4,1)S(1)} %get-tuple-element.105) | copy-start | bytes 52
  185.7 14.4 %copy-start.13 = (bf16[4,90,16,128]{3,0,2,1:T(4,128)(2,1)}, bf16[4,90,16,128]{3,0,2,1:T(4,128)(2,1)S(1)}, u32[]{:S(2)}) copy-start(bf16[4,90,16,128]{3,0,2,1:T(4,128)(2,1)S(1)} %get-tuple-element.29) | copy-start | bytes 4423684
  194.8 5.3 collective-permute-start.4
  194.9 5.2 collective-permute-start.5
  207.3 17.5 %copy-start.14 = (bf16[4,90,16,128]{3,0,2,1:T(4,128)(2,1)S(1)}, bf16[4,90,16,128]{3,0,2,1:T(4,128)(2,1)}, u32[]{:S(2)}) copy-start(bf16[4,90,16,128]{3,0,2,1:T(4,128)(2,1)} %copy-done.13) | copy-start | bytes 4423684
  208.5 13.8 %collective-permute-start.7 = (bf16[4,90,18,1]{1,0,3,2:T(4,128)(2,1)S(1)}, bf16[4,90,18,1]{1,0,3,2:T(4,128)(2,1)S(1)}, u32[]{:S(2)}, u32[]{:S(2)}) collective-permute-start(bf16[4,90,18,1]{1,0,3,2:T(4,128)(2,1)S(1)} %copy.145), channel_id=1, source_target_pairs={{1,0},{2,1},{3,2},{4,3},{5,4},{6,5},{7,6},{0,7},{9,8},{10,9},{11,1... | collective-permute-start | bytes 38888 | tf_op jit(solution)/shard_map/ppermute | solution.py:17
  213.3 6.8 %collective-permute-start.6 = (bf16[4,90,18,1]{1,0,3,2:T(4,128)(2,1)}, bf16[4,90,18,1]{1,0,3,2:T(4,128)(2,1)}, u32[]{:S(2)}, u32[]{:S(2)}) collective-permute-start(bf16[4,90,18,1]{1,0,3,2:T(4,128)(2,1)} %copy.144), channel_id=1, source_target_pairs={{0,1},{1,2},{2,3},{3,4},{4,5},{5,6},{6,7},{7,0},{8,9},{9,10},{10,1... | collective-permute-start | bytes 38888 | tf_op jit(solution)/shard_map/ppermute | solution.py:16
  272.5 25.9 %copy-start.4 = (f32[4,90,16,128]{3,0,2,1:T(4,128)}, f32[4,90,16,128]{3,0,2,1:T(4,128)S(1)}, u32[]{:S(2)}) copy-start(f32[4,90,16,128]{3,0,2,1:T(4,128)S(1)} %get-tuple-element.28) | copy-start | bytes 8847364
  281.3 5.1 collective-permute-start.8
  281.3 5.1 collective-permute-start.9
  296.3 8.9 %collective-permute-start.11 = (bf16[4,90,18,1]{1,0,3,2:T(4,128)(2,1)S(1)}, bf16[4,90,18,1]{1,0,3,2:T(4,128)(2,1)S(1)}, u32[]{:S(2)}, u32[]{:S(2)}) collective-permute-start(bf16[4,90,18,1]{1,0,3,2:T(4,128)(2,1)S(1)} %copy.153), channel_id=1, source_target_pairs={{1,0},{2,1},{3,2},{4,3},{5,4},{6,5},{7,6},{0,7},{9,8},{10,9},{11,1... | collective-permute-start | bytes 38888 | tf_op jit(solution)/shard_map/ppermute | solution.py:17
  296.4 6.6 %collective-permute-start.10 = (bf16[4,90,18,1]{1,0,3,2:T(4,128)(2,1)S(1)}, bf16[4,90,18,1]{1,0,3,2:T(4,128)(2,1)}, u32[]{:S(2)}, u32[]{:S(2)}) collective-permute-start(bf16[4,90,18,1]{1,0,3,2:T(4,128)(2,1)S(1)} %copy.152), channel_id=1, source_target_pairs={{0,1},{1,2},{2,3},{3,4},{4,5},{5,6},{6,7},{7,0},{8,9},{9,10},{10,1... | collective-permute-start | bytes 38888 | tf_op jit(solution)/shard_map/ppermute | solution.py:16
  364.4 5.4 collective-permute-start.12
  364.4 5.4 collective-permute-start.13
  379.7 9.1 %collective-permute-start.15 = (bf16[4,90,18,1]{1,0,3,2:T(4,128)(2,1)S(1)}, bf16[4,90,18,1]{1,0,3,2:T(4,128)(2,1)S(1)}, u32[]{:S(2)}, u32[]{:S(2)}) collective-permute-start(bf16[4,90,18,1]{1,0,3,2:T(4,128)(2,1)S(1)} %copy.161), channel_id=1, source_target_pairs={{1,0},{2,1},{3,2},{4,3},{5,4},{6,5},{7,6},{0,7},{9,8},{10,9},{11,1... | collective-permute-start | bytes 38888 | tf_op jit(solution)/shard_map/ppermute | solution.py:17
  379.8 6.5 %collective-permute-start.14 = (bf16[4,90,18,1]{1,0,3,2:T(4,128)(2,1)S(1)}, bf16[4,90,18,1]{1,0,3,2:T(4,128)(2,1)S(1)}, u32[]{:S(2)}, u32[]{:S(2)}) collective-permute-start(bf16[4,90,18,1]{1,0,3,2:T(4,128)(2,1)S(1)} %copy.160), channel_id=1, source_target_pairs={{0,1},{1,2},{2,3},{3,4},{4,5},{5,6},{6,7},{7,0},{8,9},{9,10},{10,1... | collective-permute-start | bytes 38888 | tf_op jit(solution)/shard_map/ppermute | solution.py:16
  399.9 22.9 %all-to-all-start.2 = ((bf16[360,8,128]{2,0,1:T(8,128)(2,1)}), bf16[360,8,128]{2,0,1:T(8,128)(2,1)}, u32[]{:S(2)}, u32[]{:S(2)}) async-start(bf16[360,8,128]{2,0,1:T(8,128)(2,1)} %get-tuple-element.97), calls=%async_computation.2 | async-start | bytes 1474560 | tf_op jit(solution)/shard_map/all_to_all | solution.py:105
  404.2 133.1 %reduce-scatter.8.cloned.1.call-start = ((), (), s32[]{:S(2)}) async-start(), calls=%async_computation.9 | async-start | bytes 921600 | tf_op jit(solution)/shard_map/reduce_scatter | solution.py:133
  428.5 23.0 %all-to-all-start.1 = ((bf16[360,8,128]{2,0,1:T(8,128)(2,1)}), bf16[360,8,128]{2,0,1:T(8,128)(2,1)}, u32[]{:S(2)}, u32[]{:S(2)}) async-start(bf16[360,8,128]{2,0,1:T(8,128)(2,1)} %fusion.20), calls=%async_computation.1 | async-start | bytes 1474560 | tf_op jit(solution)/shard_map/all_to_all | solution.py:109
  432.7 104.6 %reduce-scatter.4.cloned.1.call-start = ((), (), s32[]{:S(2)}) async-start(), calls=%async_computation.7 | async-start | bytes 921600 | tf_op jit(solution)/shard_map/reduce_scatter | solution.py:131
  451.5 38.4 %all-to-all-start.3 = ((bf16[360,8,128]{2,0,1:T(8,128)(2,1)}), bf16[360,8,128]{2,0,1:T(8,128)(2,1)}, u32[]{:S(2)}, u32[]{:S(2)}) async-start(bf16[360,8,128]{2,0,1:T(8,128)(2,1)} %fusion.18), calls=%async_computation.3 | async-start | bytes 1474560 | tf_op jit(solution)/shard_map/all_to_all | solution.py:110
  455.7 81.6 %reduce-scatter.6.cloned.1.call-start = ((), (), s32[]{:S(2)}) async-start(), calls=%async_computation.8 | async-start | bytes 1310720 | tf_op jit(solution)/shard_map/reduce_scatter | solution.py:132
  462.9 21.2 %copy-start.40 = (bf16[4,90,1,128]{3,0,2,1:T(4,128)(2,1)S(1)}, bf16[4,90,1,128]{3,0,2,1:T(4,128)(2,1)}, u32[]{:S(2)}) copy-start(bf16[4,90,1,128]{3,0,2,1:T(4,128)(2,1)} %copy-done.39) | copy-start | bytes 276484
  (55 other events, 245.3 us)
Sparse Core Ops, SparseCore 0:
  425.9 21.2 reduce-scatter.7
  450.5 22.9 reduce-scatter.3
  487.9 25.4 reduce-scatter.5
where the time goes:
time: 549 us; the launch traced here: 544 us
  local copies, waits for them, and re-layouts  315 us (57%)
  other arithmetic  100 us (18%)
  starting transfers between devices  42 us (8%)
  waiting for transfers between devices  30 us (5%)
  blocking collectives  21.2 us (4%)
  matrix products  21 us (4%)
  between operations  14.8 us (3%)
    unnamed x141, local copies, waits for them, and re-layouts  44.9 us
    broadcast_in_dim x4, local copies, waits for them, and re-layouts, shards(): east = jnp.where(lane == columns - 1, east_rim, jnp.roll(state, -1, axis=3))  42.3 us
    broadcast_in_dim x4, local copies, waits for them, and re-layouts, shards(): west = jnp.where(lane == 0, west_rim, jnp.roll(state, 1, axis=3))  42.2 us
    convert_element_type x3, other arithmetic, shards(): state.astype(jnp.bfloat16)  36.7 us
    slice x8, local copies, waits for them, and re-layouts, shards(): east = jnp.where(lane == columns - 1, east_rim, jnp.roll(state, -1, axis=3))  33.5 us
    convert_element_type x4, other arithmetic, shards(): extended(state.astype(jnp.bfloat16), (('lat', 2), ('lon', 3)), 1)  29.2 us
    slice x12, local copies, waits for them, and re-layouts, extended(): last = lax.slice_in_dim(array, length - width, length, axis=dim)  25.1 us
    slice x4, local copies, waits for them, and re-layouts, shards(): east_rim = padded[:, :, 1:-1, -1:]  21.7 us
  transfers between devices with their start and end apart: 23, of which 5 were waited for; matrix products, arithmetic and copies ran while one was open for 77% of the time, Pallas kernels for 0%

commit v1 on v0

v1 whole, which is shorter than its diff:
```python
import jax
import jax.numpy as jnp
from jax import lax
from jax.experimental import pallas as pl
from jax.experimental.pallas import tpu as pltpu
from jax.sharding import PartitionSpec as P

STEPS = 4
F32 = jnp.float32
BF16 = jnp.bfloat16
MESH = pl.DeviceIdType.MESH


def mm(a, b):
    return jnp.dot(a, b, preferred_element_type=F32)


def mm_nt(a, b):
    return lax.dot_general(a, b, (((1,), (1,)), ((), ())), preferred_element_type=F32)


def mm_tn(a, b):
    return lax.dot_general(a, b, (((0,), (0,)), ((), ())), preferred_element_type=F32)


def sigmoid(v):
    return 1.0 / (1.0 + jnp.exp(-v))


def make_kernel(nlat, nlon, nfield, levels, rows, width, hid):
    feat = nfield * levels
    ncol = rows * width
    hl = hid // nlat
    npair = nlon // 2
    nk = nlon * 128

    def kernel(
        fields, clon, clat, cdif, cot, cols, wi_t, wm_t, wo_t,
        out_f, out_a, out_gi, out_gm, out_go,
        wide, data, hot, xs, xr, ts, tr,
        wi, wm, wo, hx, hg, h1s, h2s, d1s, d2s, gs, gr,
        rim_rows, rim_lanes, got_rows, got_lanes,
        send_rows, send_lanes, recv_rows, recv_lanes,
        w_send, w_recv, x_send, x_recv, t_send, t_recv, g_send, g_recv, r_send, r_recv,
    ):
        lat = lax.axis_index("lat")
        lon = lax.axis_index("lon")
        pair_me = lon // 2

        barrier = pltpu.get_barrier_semaphore()
        for off in range(1, nlon):
            pl.semaphore_signal(
                barrier, inc=1, device_id=(lat, lax.rem(lon + off, nlon)), device_id_type=MESH
            )
        for off in range(1, nlat):
            pl.semaphore_signal(
                barrier, inc=1, device_id=(lax.rem(lat + off, nlat), lon), device_id_type=MESH
            )
        pl.semaphore_wait(barrier, nlon + nlat - 2)

        def rim_copy(step, way):
            target = (
                (lat, lax.rem(lon + nlon - 1, nlon)),
                (lat, lax.rem(lon + 1, nlon)),
                (lax.rem(lat + nlat - 1, nlat), lon),
                (lax.rem(lat + 1, nlat), lon),
            )[way]
            source, place = (
                (send_lanes, recv_lanes) if way < 2 else (send_rows, recv_rows)
            )
            return pltpu.make_async_remote_copy(
                src_ref=source.at[step, way % 2],
                dst_ref=place.at[step, way % 2],
                send_sem=r_send.at[step, way],
                recv_sem=r_recv.at[step, way],
                device_id=target,
                device_id_type=MESH,
            )

        lane = lax.broadcasted_iota(jnp.int32, (rows, width), 1)
        row = lax.broadcasted_iota(jnp.int32, (rows, width), 0)

        def keep_rims(value, c, level):
            f = c * levels + level
            here = pl.ds(c * rows, rows)
            rim_lanes[0, here, :] = jnp.where(
                lane == level, jnp.broadcast_to(value[:, :1], value.shape), rim_lanes[0, here, :]
            )
            rim_lanes[1, here, :] = jnp.where(
                lane == level + 1,
                jnp.broadcast_to(value[:, width - 1 :], value.shape),
                rim_lanes[1, here, :],
            )
            rim_rows[0, pl.ds(f, 1), :] = value[:1, :]
            rim_rows[1, pl.ds(f, 1), :] = value[rows - 1 :, :]

        def send_rims(step):
            send_lanes[step] = rim_lanes[...].astype(BF16)
            send_rows[step] = rim_rows[...].astype(BF16)
            for way in range(4):
                rim_copy(step, way).start()

        rim_lanes[...] = jnp.zeros_like(rim_lanes)
        rim_rows[...] = jnp.zeros_like(rim_rows)

        @pl.loop(0, levels)
        def _(level):
            for c in range(nfield):
                keep_rims(
                    fields[pl.ds(pl.multiple_of((c * levels + level) * rows, rows), rows), :],
                    c,
                    level,
                )

        send_rims(0)

        full_w = (wi, wm, wo)
        own_w = (wi_t, wm_t, wo_t)
        place_w = pl.ds(pl.multiple_of(lat * hl, hl), hl)

        def weight_copy(which, off):
            other = lax.rem(lat + off, nlat)
            return pltpu.make_async_remote_copy(
                src_ref=own_w[which],
                dst_ref=full_w[which].at[place_w, :],
                send_sem=w_send.at[which, off],
                recv_sem=w_recv.at[which, off],
                device_id=(other, lon),
                device_id_type=MESH,
            )

        for which in range(3):
            for off in range(1, nlat):
                weight_copy(which, off).start()
            full_w[which][place_w, :] = own_w[which][...]

        wide[...] = cot[...].astype(F32)
        for r in range(rows):
            part = jnp.concatenate(
                [
                    fields[pl.ds(r, feat, stride=rows), :],
                    wide[pl.ds(r, feat, stride=rows), :],
                ],
                axis=0,
            )
            data[:, r * width : (r + 1) * width] = part.astype(BF16)

        def block_copy(source, place, sends, recvs, other):
            return pltpu.make_async_remote_copy(
                src_ref=source.at[other],
                dst_ref=place.at[lon],
                send_sem=sends.at[other],
                recv_sem=recvs.at[lon],
                device_id=(lat, other),
                device_id_type=MESH,
            )

        def block_wait(source, place, sends, recvs, other):
            return pltpu.make_async_remote_copy(
                src_ref=source.at[other],
                dst_ref=place.at[other],
                send_sem=sends.at[other],
                recv_sem=recvs.at[other],
                device_id=(lat, other),
                device_id_type=MESH,
            )

        def ship(source, place, sends, recvs, other):
            @pl.when(other != lon)
            def _():
                block_copy(source, place, sends, recvs, other).start()

            @pl.when(other == lon)
            def _():
                place[lon] = source[lon]

        def arrive(source, place, sends, recvs, other):
            @pl.when(other != lon)
            def _():
                block_wait(source, place, sends, recvs, other).wait_recv()

        @pl.loop(0, npair)
        def _(i):
            p = lax.rem(pair_me + 1 + i, npair)
            at = pl.ds(pl.multiple_of(p * 256, 256), 256)
            names = cols[:, at]
            index = lax.broadcasted_iota(jnp.int32, (ncol, 256), 0)
            hot[:, at] = jnp.where(index == names, 1.0, 0.0).astype(BF16)
            picked = mm(data[...], hot[:, at]).astype(BF16)
            for half in range(2):
                xs[2 * p + half] = picked[:, half * 128 : (half + 1) * 128]
                ship(xs, xr, x_send, x_recv, 2 * p + half)

        top = (lat < nlat - 1).astype(F32)
        bottom = (lat > 0).astype(F32)

        def dynamics(step):
            for way in range(4):
                rim_copy(step, way).wait_recv()
            got_lanes[...] = recv_lanes[step].astype(F32)
            got_rows[0] = recv_rows[step, 0].astype(F32) * top
            got_rows[1] = recv_rows[step, 1].astype(F32) * bottom
            origin = fields if step == 0 else out_f

            @pl.loop(0, levels)
            def _(level):
                flat = pl.ds(pl.multiple_of(level * rows, rows), rows)
                half_lon = 0.5 * clon[flat, :]
                half_lat = 0.5 * clat[flat, :]
                dif = cdif[flat, :]
                c_here = 1.0 - 4.0 * dif
                c_east, c_west = dif - half_lon, dif + half_lon
                c_north, c_south = dif - half_lat, dif + half_lat
                for c in range(nfield):
                    f = c * levels + level
                    at = pl.ds(pl.multiple_of(f * rows, rows), rows)
                    here = pl.ds(c * rows, rows)
                    v = origin[at, :]
                    shift = width - 1 - level
                    east = jnp.where(
                        lane == width - 1,
                        pltpu.roll(got_lanes[0, here, :], shift, 1),
                        pltpu.roll(v, width - 1, 1),
                    )
                    west = jnp.where(
                        lane == 0,
                        pltpu.roll(got_lanes[1, here, :], shift, 1),
                        pltpu.roll(v, 1, 1),
                    )
                    north = jnp.where(
                        row == rows - 1,
                        jnp.broadcast_to(got_rows[0, pl.ds(f, 1), :], v.shape),
                        pltpu.roll(v, rows - 1, 0),
                    )
                    south = jnp.where(
                        row == 0,
                        jnp.broadcast_to(got_rows[1, pl.ds(f, 1), :], v.shape),
                        pltpu.roll(v, 1, 0),
                    )
                    new = (
                        c_here * v + c_east * east + c_west * west + c_north * north + c_south * south
                    )
                    out_f[at, :] = new
                    if step < STEPS - 1:
                        keep_rims(new, c, level)

            if step < STEPS - 1:
                send_rims(step + 1)

        dynamics(0)
        dynamics(1)
        dynamics(2)

        for which in range(3):
            for off in range(1, nlat):
                weight_copy(which, off).wait_recv()

        @pl.loop(0, npair)
        def _(i):
            p = lax.rem(pair_me + npair - i, npair)
            at = pl.ds(pl.multiple_of(p * 256, 256), 256)
            for half in range(2):
                arrive(xs, xr, x_send, x_recv, 2 * p + half)
            both = jnp.concatenate([xr[2 * p], xr[2 * p + 1]], axis=1).astype(F32)
            x = both[:feat]
            g = both[feat:].astype(BF16)
            scale = lax.rsqrt(jnp.mean(x * x, axis=0, keepdims=True) + 1e-06)
            xn = (x * scale).astype(BF16)
            hx[:, at] = xn
            hg[:, at] = g
            a1 = mm(wi[...], xn)
            s1 = sigmoid(a1)
            h1 = (a1 * s1).astype(BF16)
            h1s[:, at] = h1
            a2 = mm(wm[...], h1)
            s2 = sigmoid(a2)
            h2 = (a2 * s2).astype(BF16)
            h2s[:, at] = h2
            tend = mm_tn(wo[...], h2)
            d2 = (mm(wo[...], g) * (s2 * (1.0 + a2 * (1.0 - s2)))).astype(BF16)
            d2s[:, at] = d2
            d1 = (mm_tn(wm[...], d2) * (s1 * (1.0 + a1 * (1.0 - s1)))).astype(BF16)
            d1s[:, at] = d1
            dxn = mm_tn(wi[...], d1)
            adj = scale * dxn - x * (scale * scale * scale) * jnp.mean(x * dxn, axis=0, keepdims=True)
            back = jnp.concatenate([tend, adj], axis=0).astype(BF16)
            for half in range(2):
                ts[2 * p + half] = back[:, half * 128 : (half + 1) * 128]
                ship(ts, tr, t_send, t_recv, 2 * p + half)

        def partial(owner):
            at = pl.ds(pl.multiple_of(owner * hl, hl), hl)
            return (
                mm_nt(hx[...], d1s[at, :]),
                mm_nt(h1s[...], d2s[at, :]),
                mm_nt(hg[...], h2s[at, :]),
            )

        def grad_copy(off):
            other = lax.rem(lat + off, nlat)
            return pltpu.make_async_remote_copy(
                src_ref=gs.at[off],
                dst_ref=gr.at[off],
                send_sem=g_send.at[off],
                recv_sem=g_recv.at[off],
                device_id=(other, lon),
                device_id_type=MESH,
            )

        @pl.loop(1, nlat)
        def _(off):
            gs[off] = jnp.concatenate(partial(lax.rem(lat + off, nlat)), axis=0).astype(BF16)
            grad_copy(off).start()

        out_gi[...], out_gm[...], out_go[...] = partial(lat)

        dynamics(3)

        @pl.loop(0, nlon)
        def _(e):
            arrive(ts, tr, t_send, t_recv, e)
            data[:, pl.ds(pl.multiple_of(e * 128, 128), 128)] = tr[e]

        for q in range(rows // 2):
            spread = mm_nt(data[:, :nk], hot[q * 256 : (q + 1) * 256, :])
            for half in range(2):
                at = pl.ds(2 * q + half, feat, stride=rows)
                block = spread[:, half * 128 : (half + 1) * 128]
                out_f[at, :] = out_f[at, :] + block[:feat]
                wide[at, :] = block[feat:]
        out_a[...] = wide[...].astype(BF16)

        @pl.loop(1, nlat)
        def _(off):
            grad_copy(off).wait_recv()
            total = gr[off].astype(F32)
            out_gi[...] += total[:feat]
            out_gm[...] += total[feat : feat + hid]
            out_go[...] += total[feat + hid :]

        for step in range(STEPS):
            for way in range(4):
                rim_copy(step, way).wait_send()
        for which in range(3):
            for off in range(1, nlat):
                weight_copy(which, off).wait_send()
        for off in range(1, nlat):
            grad_copy(off).wait_send()

        @pl.loop(0, nlon)
        def _(e):
            @pl.when(e != lon)
            def _():
                block_copy(xs, xr, x_send, x_recv, e).wait_send()
                block_copy(ts, tr, t_send, t_recv, e).wait_send()

    def vm(*shape, dtype=BF16):
        return pltpu.VMEM(shape, dtype)

    frows = (feat + 15) // 16 * 16
    dma = pltpu.SemaphoreType.DMA
    scratch = [
        vm(feat * rows, width, dtype=F32),
        vm(2 * feat, ncol),
        vm(ncol, nk),
        vm(nlon, 2 * feat, 128), vm(nlon, 2 * feat, 128),
        vm(nlon, 2 * feat, 128), vm(nlon, 2 * feat, 128),
        vm(hid, feat), vm(hid, hid), vm(hid, feat),
        vm(feat, nk), vm(feat, nk),
        vm(hid, nk), vm(hid, nk), vm(hid, nk), vm(hid, nk),
        vm(nlat, 2 * feat + hid, hl), vm(nlat, 2 * feat + hid, hl),
        vm(2, frows, width, dtype=F32), vm(2, nfield * rows, width, dtype=F32),
        vm(2, frows, width, dtype=F32), vm(2, nfield * rows, width, dtype=F32),
        vm(STEPS, 2, frows, width), vm(STEPS, 2, nfield * rows, width),
        vm(STEPS, 2, frows, width), vm(STEPS, 2, nfield * rows, width),
        dma((3, nlat)), dma((3, nlat)),
        dma((nlon,)), dma((nlon,)), dma((nlon,)), dma((nlon,)),
        dma((nlat,)), dma((nlat,)),
        dma((STEPS, 4)), dma((STEPS, 4)),
    ]
    outs = [
        jax.ShapeDtypeStruct((feat * rows, width), F32),
        jax.ShapeDtypeStruct((feat * rows, width), BF16),
        jax.ShapeDtypeStruct((feat, hl), F32),
        jax.ShapeDtypeStruct((hid, hl), F32),
        jax.ShapeDtypeStruct((feat, hl), F32),
    ]
    return pl.pallas_call(
        kernel,
        out_shape=outs,
        in_specs=[pl.BlockSpec(memory_space=pltpu.VMEM)] * 9,
        out_specs=[pl.BlockSpec(memory_space=pltpu.VMEM)] * 5,
        scratch_shapes=scratch,
        compiler_params=pltpu.CompilerParams(
            collective_id=0, has_side_effects=True, vmem_limit_bytes=62 * 2**20
        ),
        name="window",
    )


def shards(
    fields, courant_lon, courant_lat, diffusion, tend_cot,
    col_list, block_count, block_dest, w_in, w_mid, w_out,
):
    nfield, levels, rows, width = fields.shape
    nlat, nlon = lax.axis_size("lat"), lax.axis_size("lon")
    hid = w_mid.shape[1]
    nblock = block_dest.shape[-1]
    block_len = col_list.shape[-1] // nblock
    dest = block_dest.reshape(nblock)
    counts = block_count.reshape(nblock)
    slot = jnp.arange(block_len, dtype=jnp.int32)
    named = jnp.where(
        slot[None, :] < counts[:, None], col_list.reshape(nblock, block_len), rows * width
    )
    mine = dest[None, :] == jnp.arange(nblock, dtype=jnp.int32)[:, None]
    cols = jnp.sum(jnp.where(mine[:, :, None], named[None], 0), axis=1).reshape(1, -1)
    flat = lambda a: a.reshape(-1, width)
    new, adj, gi, gm, go = make_kernel(nlat, nlon, nfield, levels, rows, width, hid)(
        flat(fields), flat(courant_lon), flat(courant_lat), flat(diffusion), flat(tend_cot),
        cols, w_in[0].T, w_mid[0].T, w_out[0].T,
    )
    return (new.reshape(fields.shape), adj.reshape(fields.shape), gi[None], gm[None], go[None])


def solution(mesh):
    tile = P(None, None, "lat", "lon")
    plane = P(None, "lat", "lon")
    table = P("lat", "lon", None)
    weight = P("lon", None, "lat")
    return jax.shard_map(
        shards,
        mesh=mesh,
        in_specs=(tile, plane, plane, plane, tile, table, table, table, weight, weight, weight),
        out_specs=(tile, tile, weight, weight, weight),
        check_vma=False,
    )
```

time: 549 us -> 152 us (0.28)
  local copies, waits for them, and re-layouts: 315 us -> 11.8 us
  Pallas kernels: 0 us -> 135 us
  other arithmetic: 100 us -> 2.1 us
  starting transfers between devices: 42 us -> 0 us
  waiting for transfers between devices: 30 us -> 0 us
  blocking collectives: 21.2 us -> 0 us
  matrix products: 21 us -> 0 us
  between operations: 14.8 us -> 0.66 us
    pallas_call x0 -> x1, Pallas kernels: none -> 135 us  [shards(): make_kernel(nlat, nlon, nfield, levels, rows, width, hid)]
    slice x36 -> x0, local copies, waits for them, and re-layouts: 107 us -> none  [the longest x8 33.5 us: shards(): east = jnp.where(lane == columns - 1, east_rim, jnp.roll(state, -1, axis=3))]
    broadcast_in_dim x8 -> x0, local copies, waits for them, and re-layouts: 84.6 us -> none  [the longest x4 42.3 us: shards(): east = jnp.where(lane == columns - 1, east_rim, jnp.roll(state, -1, axis=3))]
    convert_element_type x8 -> x0, other arithmetic: 68.3 us -> none  [the longest x3 36.7 us: shards(): state.astype(jnp.bfloat16)]
    unnamed x141 -> x16, local copies, waits for them, and re-layouts: 44.9 us -> 11.8 us
    ppermute x8 -> x0, local copies, waits for them, and re-layouts: 28.4 us -> none  [the longest x4 18.4 us: extended(): before = lax.ppermute(last, axis, up)]
    ppermute x16 -> x0, starting transfers between devices: 22.4 us -> none  [the longest x8 17.7 us: extended(): after = lax.ppermute(first, axis, down)]
    all_gather x3 -> x0, blocking collectives: 21.2 us -> none  [the longest x1 8 us: shards(): lax.all_gather(w_mid, 'lat', axis=2, tiled=True)]
  transfers between devices with their start and end apart: 23 -> 0, of which waited for: 5 -> 0; matrix products, arithmetic and copies ran while one was open for 77% -> 0% of each run, Pallas kernels for 0% -> 0%
where the time goes in v1:
time: 152 us; the launch traced here: 149 us
  Pallas kernels  135 us (89%)
  local copies, waits for them, and re-layouts  11.8 us (8%)
  other arithmetic  2.1 us (1%)
    pallas_call x1, Pallas kernels, shards(): make_kernel(nlat, nlon, nfield, levels, rows, width, hid)  135 us
    unnamed x16, local copies, waits for them, and re-layouts  11.8 us

profile of v1, /device:TPU:0, one launch (start us, length us, event | category | flops | bytes accessed | tf_op | source)
XLA Modules:
  0.0 149.4 jit_solution(12262475428148669961)
XLA Ops:
  0.6 0.7 iota_compare_fusion.1
  1.3 0.8 fusion
  2.1 0.7 select_reduce_fusion
  2.7 1.6 %copy.19 = bf16[1,360,128]{1,2,0:T(8,128)(2,1)} copy(bf16[1,360,128]{2,1,0:T(8,128)(2,1)} %param.19) | data formatting | bytes 184320 | tf_op args[8]
  4.4 1.6 %copy.21 = bf16[1,360,128]{1,2,0:T(8,128)(2,1)} copy(bf16[1,360,128]{2,1,0:T(8,128)(2,1)} %param.21) | data formatting | bytes 184320 | tf_op args[10]
  6.0 1.7 %copy.20 = bf16[1,512,128]{1,2,0:T(8,128)(2,1)} copy(bf16[1,512,128]{2,1,0:T(8,128)(2,1)} %param.20) | data formatting | bytes 262144 | tf_op args[9]
  7.7 134.8 %window.1 = (f32[5760,128]{1,0:T(8,128)}, bf16[5760,128]{1,0:T(8,128)(2,1)}, f32[360,128]{1,0:T(8,128)}, f32[512,128]{1,0:T(8,128)}, f32[360,128]{1,0:T(8,128)}) custom-call(f32[5760,128]{1,0:T(8,128)} %bitcast.23, f32[1440,128]{1,0:T(8,128)} %bitcast.27, f32[1440,128]{1,0:T(8,128)} %bitcast.28, f32[1440,128]{1,0:T(8,128)} %bitcast.29, ...), custom_call_target="tpu_custom_call" | custom-call | tf_op jit(solution)/shard_map/window/pallas_call | solution.py:419
  142.5 0.0 copy-start
  142.5 0.0 copy-start.3
  142.5 3.7 %copy.27 = f32[4,90,16,128]{3,2,1,0:T(8,128)} copy(f32[4,90,16,128]{3,2,1,0:T(8,128)} %bitcast.24) | data formatting | bytes 5898240
  146.2 0.0 copy-done
  146.2 0.0 copy-start.1
  146.2 0.0 copy-start.2
  146.2 1.1 copy.28
  147.3 0.0 copy-done.3
  147.3 0.7 copy.29
  148.0 0.0 copy-done.1
  148.0 0.7 copy.30
  148.7 0.0 copy-done.2
  148.7 0.7 copy.31
Async XLA Ops:
  142.5 3.8 %copy-start = (bf16[5760,128]{1,0:T(8,128)(2,1)S(1)}, bf16[5760,128]{1,0:T(8,128)(2,1)}, u32[]{:S(2)}) copy-start(bf16[5760,128]{1,0:T(8,128)(2,1)} %get-tuple-element.11) | copy-start | bytes 4423684
  142.5 4.9 %copy-start.3 = (f32[360,128]{1,0:T(8,128)S(1)}, f32[360,128]{1,0:T(8,128)}, u32[]{:S(2)}) copy-start(f32[360,128]{1,0:T(8,128)} %get-tuple-element.12) | copy-start | bytes 552964
  146.2 1.8 %copy-start.1 = (f32[512,128]{1,0:T(8,128)S(1)}, f32[512,128]{1,0:T(8,128)}, u32[]{:S(2)}) copy-start(f32[512,128]{1,0:T(8,128)} %get-tuple-element.13) | copy-start | bytes 786436
  146.2 2.5 %copy-start.2 = (f32[360,128]{1,0:T(8,128)S(1)}, f32[360,128]{1,0:T(8,128)}, u32[]{:S(2)}) copy-start(f32[360,128]{1,0:T(8,128)} %get-tuple-element.14) | copy-start | bytes 552964
